TPU v7x, 32 devices: a whole 2x2x4 slice. The times are simulated.
32 devices in a mesh: ctx: 8 (over y, x, core), head: 4 (over z).
Axes of the slice: x: 2, y: 2, z: 4, core: 2. Of those that a mesh axis runs over, the one named last changes fastest.
Arguments:
- queries: bfloat16 [2, 4096, 2560], P(None, ('ctx', 'head')), may hold values from -6 to 6
- keys: bfloat16 [2, 4096, 2560], P(None, ('ctx', 'head')), may hold values from -6 to 6
- values: bfloat16 [2, 4096, 2560], P(None, ('ctx', 'head')), may hold values from -6 to 6
- rates: bfloat16 [2, 4096, 4], P(None, ('ctx', 'head')), may hold values from 0.00018501282 to 0.0018463135
- gate_fast: float32 [4, 640, 640], P('head'), may hold values from -0.25 to 0.25
- up_fast: float32 [4, 640, 640], P('head'), may hold values from -0.25 to 0.25
- down_fast: float32 [4, 640, 640], P('head'), may hold values from -0.25 to 0.25
- out_gain: float32 [2560], P('head'), may hold values from 0.5 to 1.5
- out_proj: bfloat16 [2560, 2560], P('head'), may hold values from -0.125 to 0.125
Outputs:
- mixed: bfloat16 [2, 4096, 2560], P(None, ('ctx', 'head'))
All inputs are finite; a program needn't handle non-finite values.
Results may differ from a plain program's by a relative error of at most 0.014.
Values may be sent and summed in bfloat16 or wider, within the bound.
A program may use at most 128 MiB of HBM per device.

v0:
```python
import functools

import jax
import jax.numpy as jnp
from jax import lax
from jax.experimental import pallas as pl
from jax.experimental.pallas import tpu as pltpu
from jax.sharding import PartitionSpec as P

bf16 = jnp.bfloat16
f32 = jnp.float32
MESH = pl.DeviceIdType.MESH
NN = (((1,), (0,)), ((), ()))
NT = (((1,), (1,)), ((), ()))
TN = (((0,), (0,)), ((), ()))
TILE = 128


def dot(left, right, dims):
    return lax.dot_general(left, right, dims, preferred_element_type=f32)


def dot_split(left, right, dims):
    high = left.astype(bf16)
    low = (left - high.astype(f32)).astype(bf16)
    return dot(high, right, dims) + dot(low, right, dims)


def kernel(
    n_ctx, n_head, rows,
    q_ref, k_ref, v_ref, r_ref, g_ref, u_ref, d_ref, gain_ref,
    o_ref,
    tgt, kx, tx, qx, wb, wt, mst, gb, rb1, sb, rb2, dgu, hid, nrm,
    tok_send, tok_recv, tok_local, rs1_s, rs1_r, rs2_s, rs2_r, ag_s, ag_r, sib_s, sib_r,
):
    blocks, share, _ = q_ref.shape
    width = g_ref.shape[1]
    chips = n_ctx // 2
    half = chips * rows
    me_c, me_z = lax.axis_index("ctx"), lax.axis_index("head")
    core, chip = lax.rem(me_c, 2), me_c // 2
    sibling = me_c + 1 - 2 * core

    def mate(step):
        return lax.rem(chip + step, chips) * 2 + core

    def peer(step):
        return lax.rem(me_z + step, n_head)

    barrier = pltpu.get_barrier_semaphore()
    for step in range(1, n_head):
        pl.semaphore_signal(barrier, inc=1, device_id={"head": peer(step)}, device_id_type=MESH)
    for step in range(1, chips):
        pl.semaphore_signal(barrier, inc=1, device_id={"ctx": mate(step)}, device_id_type=MESH)
    pl.semaphore_signal(barrier, inc=1, device_id={"ctx": sibling}, device_id_type=MESH)
    pl.semaphore_wait(barrier, n_head - 1 + chips)

    def columns(head):
        return pl.ds(pl.multiple_of(head * width, TILE), width)

    def remote(src, dst, send, recv, device):
        copy = pltpu.make_async_remote_copy(
            src_ref=src, dst_ref=dst, send_sem=send, recv_sem=recv, device_id=device, device_id_type=MESH
        )
        copy.start()
        return copy

    def spread(kind, block, source, landing):
        copies = []
        for step in range(1, n_head):
            copies.append(remote(
                source.at[block, :, columns(peer(step))], landing.at[block, me_z],
                tok_send.at[kind, block, step], tok_recv.at[kind, block, step], {"head": peer(step)},
            ))
        local = pltpu.make_async_copy(
            source.at[block, :, columns(me_z)], landing.at[block, me_z], tok_local.at[kind, block]
        )
        local.start()
        return copies, local

    def sent(copies):
        for copy in copies[0]:
            copy.wait_send()

    def arrived(copies):
        for copy in copies[0]:
            copy.wait_recv()
        copies[1].wait()

    def scale_values(block):
        for head in range(n_head):
            cols = slice(head * width, (head + 1) * width)
            rate = r_ref[block, :, head:head + 1].astype(f32)
            tgt[block, :, cols] = (v_ref[block, :, cols].astype(f32) * rate).astype(bf16)

    def grads(block):
        def chunk(z, carry):
            at = pl.ds(pl.multiple_of(z * share, 16), share)
            pre = dot(kx[block, z], wb[block, :2 * width, :], NT)
            pre_gate, pre_up = pre[:, :width], pre[:, width:]
            sigma = jax.nn.sigmoid(pre_gate)
            silu = pre_gate * sigma
            hid[at, :] = silu * pre_up
            back = dot(tx[block, z], wb[block, 2 * width:3 * width, :], NN)
            dgu[at, :width] = back * pre_up * sigma * (1.0 + pre_gate * (1.0 - sigma))
            dgu[at, width:] = back * silu
            return carry

        lax.fori_loop(0, n_head, chunk, 0)
        keys = kx[block].reshape(n_head * share, width)

        def key_tile(i, carry):
            at = pl.ds(pl.multiple_of(i * TILE, TILE), TILE)
            gb[block, at, :] = dot_split(dgu[:, at], keys, TN).astype(bf16)
            return carry

        lax.fori_loop(0, 2 * width // TILE, key_tile, 0)
        targets = tx[block].reshape(n_head * share, width)

        def down_tile(i, carry):
            at = pl.ds(pl.multiple_of(i * TILE, TILE), TILE)
            to = pl.ds(pl.multiple_of(2 * width + i * TILE, TILE), TILE)
            high = hid[...].astype(bf16)
            low = (hid[...] - high.astype(f32)).astype(bf16)
            tile = tx[block, :, :, at].reshape(n_head * share, TILE)
            gb[block, to, :] = (dot(tile, high, TN) + dot(tile, low, TN)).astype(bf16)
            return carry

        lax.fori_loop(0, width // TILE, down_tile, 0)
        if n_ctx * rows > 3 * width:
            gb[block, 3 * width:, :] = jnp.zeros((n_ctx * rows - 3 * width, width), bf16)

    def shard(of_core, of_chip):
        return pl.ds(pl.multiple_of((of_core * chips + of_chip) * rows, 16), rows)

    mine = shard(core, chip)
    pending = []

    def reduce_start(block):
        first = {}
        for step in list(range(1, chips)) + [0]:
            other = lax.rem(chip + step, chips)
            first[step] = remote(
                gb.at[block, shard(1 - core, other)], rb1.at[block, step],
                rs1_s.at[block, step], rs1_r.at[block, step], {"ctx": sibling},
            )
        second = []
        for step in range(1, chips):
            other = lax.rem(chip + step, chips)
            first[step].wait_recv()
            pair = gb[block, shard(core, other), :].astype(f32) + rb1[block, step].astype(f32)
            sb[block, step] = pair.astype(bf16)
            second.append(remote(
                sb.at[block, step], rb2.at[block, step],
                rs2_s.at[block, step], rs2_r.at[block, step], {"ctx": mate(step)},
            ))
        pending.extend(first.values())
        pending.extend(second)
        return first[0], second

    def reduce_finish(block, state, norm):
        own, second = state
        own.wait_recv()
        total = gb[block, mine, :].astype(f32) + rb1[block, 0].astype(f32)
        for step, copy in enumerate(second):
            copy.wait_recv()
            total = total + rb2[block, step + 1].astype(f32)
        fresh = mst[...] + total
        fresh = fresh * (norm * lax.rsqrt(jnp.sum(fresh * fresh, axis=1, keepdims=True) + 1e-06))
        mst[...] = fresh
        wb[block + 1, mine, :] = fresh.astype(bf16)
        out = [
            remote(
                wb.at[block + 1, mine], wb.at[block + 1, mine],
                ag_s.at[block, step], ag_r.at[block, step], {"ctx": mate(step)},
            )
            for step in range(1, chips)
        ]
        pair = [remote(
            wb.at[block + 1, mine], wb.at[block + 1, mine], sib_s.at[block, 0], sib_r.at[block, 0], {"ctx": sibling}
        )]
        return out, pair

    def share_finish(block, state):
        out, pair = state
        for step, copy in enumerate(out):
            copy.wait_recv()
            origin = shard(core, lax.rem(chip + chips - step - 1, chips))
            pair.append(remote(
                wb.at[block + 1, origin], wb.at[block + 1, origin],
                sib_s.at[block, step + 1], sib_r.at[block, step + 1], {"ctx": sibling},
            ))
        for copy in pair:
            copy.wait_recv()
        pending.extend(out)
        pending.extend(pair)

    def apply(block):
        def chunk(z, carry):
            at = pl.ds(pl.multiple_of(z * share, 16), share)
            pre = dot(qx[block, z], wb[block + 1, :2 * width, :], NT)
            pre_gate = pre[:, :width]
            hidden = pre_gate * jax.nn.sigmoid(pre_gate) * pre[:, width:]
            out = dot_split(hidden, wb[block + 1, 2 * width:3 * width, :], NT)
            scale = lax.rsqrt(jnp.mean(out * out, axis=-1, keepdims=True) + 1e-05)
            nrm[block, at, :] = (out * scale * gain_ref[...]).astype(bf16)
            return carry

        lax.fori_loop(0, n_head, chunk, 0)
        copies = []
        for step in range(1, n_head):
            at = pl.ds(pl.multiple_of(peer(step) * share, 16), share)
            copies.append(remote(
                nrm.at[block, at], o_ref.at[block, :, columns(me_z)],
                tok_send.at[3, block, step], tok_recv.at[3, block, step], {"head": peer(step)},
            ))
        at = pl.ds(pl.multiple_of(me_z * share, 16), share)
        local = pltpu.make_async_copy(
            nrm.at[block, at], o_ref.at[block, :, columns(me_z)], tok_local.at[3, block]
        )
        local.start()
        return copies, local

    key_sends = [spread(0, 0, k_ref, kx)]
    scale_values(0)
    tgt_sends = [spread(1, 0, tgt, tx)]
    for block in range(1, blocks):
        scale_values(block)
    for index, ref in enumerate((g_ref, u_ref, d_ref)):
        def turn(i, carry, ref=ref, index=index):
            at = pl.ds(pl.multiple_of(i * TILE, TILE), TILE)
            to = pl.ds(pl.multiple_of(index * width + i * TILE, TILE), TILE)
            tile = ref[0, :, at].T
            wt[to, :] = tile
            wb[0, to, :] = tile.astype(bf16)
            return carry

        lax.fori_loop(0, width // TILE, turn, 0)
    if n_ctx * rows > 3 * width:
        wt[3 * width:, :] = jnp.zeros((n_ctx * rows - 3 * width, width), f32)
    mst[...] = wt[mine, :]
    norm = jnp.sqrt(jnp.sum(mst[...] * mst[...], axis=1, keepdims=True))

    query_sends, results = [], []
    for block in range(blocks):
        ahead = block + 1 < blocks
        if ahead:
            sent(key_sends[block])
            key_sends.append(spread(0, block + 1, k_ref, kx))
        arrived(key_sends[block])
        if ahead:
            sent(tgt_sends[block])
            tgt_sends.append(spread(1, block + 1, tgt, tx))
        arrived(tgt_sends[block])
        grads(block)
        state = reduce_start(block)
        if block > 0:
            arrived(query_sends[block - 1])
            results.append(apply(block - 1))
        state = reduce_finish(block, state, norm)
        query_sends.append(spread(2, block, q_ref, qx))
        share_finish(block, state)
    sent(key_sends[-1])
    sent(tgt_sends[-1])
    arrived(query_sends[-1])
    results.append(apply(blocks - 1))
    for copies in query_sends:
        sent(copies)
    for copies in results:
        arrived(copies)
        sent(copies)
    for copy in pending:
        copy.wait_send()


def gather_proj(out_proj):
    cols = out_proj.shape[1] // lax.axis_size("ctx")
    piece = lax.dynamic_slice_in_dim(out_proj, lax.axis_index("ctx") * cols, cols, 1)
    piece = lax.all_gather(piece, "head", axis=0, tiled=True)
    return lax.all_gather(piece, "ctx", axis=1, tiled=True)


def per_device(queries, keys, values, rates, gate_fast, up_fast, down_fast, out_gain, out_proj):
    blocks, share, _ = queries.shape
    width = gate_fast.shape[1]
    n_ctx, n_head = lax.axis_size("ctx"), lax.axis_size("head")
    chips = n_ctx // 2
    rows = -(-3 * width // (16 * n_ctx)) * 16
    dma = pltpu.SemaphoreType.DMA
    landing = pltpu.VMEM((blocks, n_head, share, width), bf16)
    exchange = pltpu.VMEM((blocks, chips, rows, width), bf16)
    vmem = pl.BlockSpec(memory_space=pltpu.VMEM)
    anywhere = pl.BlockSpec(memory_space=pl.ANY)
    proj = gather_proj(out_proj)
    normed = pl.pallas_call(
        functools.partial(kernel, n_ctx, n_head, rows),
        out_shape=jax.ShapeDtypeStruct(queries.shape, bf16),
        in_specs=[anywhere] * 2 + [vmem] * 6,
        out_specs=vmem,
        scratch_shapes=[
            pltpu.VMEM(values.shape, bf16),
            landing, landing, landing,
            pltpu.VMEM((blocks + 1, n_ctx * rows, width), bf16),
            pltpu.VMEM((n_ctx * rows, width), f32),
            pltpu.VMEM((rows, width), f32),
            pltpu.VMEM((blocks, n_ctx * rows, width), bf16),
            exchange, exchange, exchange,
            pltpu.VMEM((n_head * share, 2 * width), f32),
            pltpu.VMEM((n_head * share, width), f32),
            pltpu.VMEM((blocks, n_head * share, width), bf16),
            dma((4, blocks, n_head)), dma((4, blocks, n_head)), dma((4, blocks)),
        ] + [dma((blocks, chips))] * 8,
        compiler_params=pltpu.CompilerParams(
            collective_id=0, has_side_effects=True, vmem_limit_bytes=60 * 1024 * 1024
        ),
        cost_estimate=pl.CostEstimate(flops=20_000_000_000, bytes_accessed=300_000_000, transcendentals=0),
    )(queries, keys, values, rates, gate_fast, up_fast, down_fast, out_gain[None, :])
    return jnp.einsum("btf,fd->btd", normed, proj, preferred_element_type=f32).astype(bf16)


def solution(mesh):
    tokens = P(None, ("ctx", "head"), None)
    matrix = P("head", None, None)
    return jax.shard_map(
        per_device,
        mesh=mesh,
        in_specs=(tokens,) * 4 + (matrix,) * 3 + (P("head"), P("head", None)),
        out_specs=tokens,
        check_vma=False,
    )
```

profile of v0, /device:TPU:26, one launch (start us, length us, event | category | flops | bytes accessed | tf_op | source)
XLA Modules:
  0.0 240.6 jit_solution(4898313342406703149)
XLA Ops:
  6.5 0.0 copy-start
  6.5 0.0 all-gather.3.cloned.1.call-start
  6.5 1.9 copy-done
  8.5 1.0 constant_dynamic-slice_fusion
  9.5 0.0 copy-start.1
  9.5 0.0 copy-start.2
  9.5 2.0 copy.12
  11.5 0.0 all-gather.3.cloned.1.call-update
  11.5 0.0 all-gather.5.cloned.1.call-start
  11.5 37.1 %all-gather.3.cloned.1.call-done = bf16[2560,320]{0,1:T(8,128)(2,1)} async-done(((bf16[640,320]{0,1:T(8,128)(2,1)}), bf16[2560,320]{0,1:T(8,128)(2,1)}) %all-gather.3.cloned.1.call-update) | async-done | bytes 1638416 | tf_op jit(solution)/shard_map/all_gather | solution.py:279
  48.7 0.0 all-gather.5.cloned.1.call-update
  48.7 0.0 copy-done.1
  48.7 0.6 broadcast_in_dim.3.gain_ref
  49.3 0.0 copy-done.2
  49.3 0.8 copy.10.r_ref
  50.1 173.9 %shard_map.91 = bf16[2,128,2560]{2,1,0:T(8,128)(2,1)} custom-call(bf16[2,128,2560]{2,1,0:T(8,128)(2,1)} %q_ref.1, bf16[2,128,2560]{2,1,0:T(8,128)(2,1)} %k_ref.1, bf16[2,128,2560]{2,1,0:T(8,128)(2,1)} %v_ref.1, bf16[2,128,4]{2,1,0:T(8,128)(2,1)} %copy.10.r_ref, f32[1,640,640]{2,1,0:T(8,128)} %g_ref.1, f32[1,640,640]{2,1,0:T(8,128)} %u_ref.1, ...), custom_call_target="tpu_custom_call" | custom-call | flops 20000000000 | bytes 300000000 | tf_op jit(solution)/shard_map/pallas_call | solution.py:295
  223.9 0.0 all-gather.5.cloned.1.call-done
  224.0 9.8 %fusion.2 = bf16[2,128,2560]{2,1,0:T(8,128)(2,1)} fusion(bf16[2,128,2560]{2,1,0:T(8,128)(2,1)} %shard_map.91, bf16[2560,2560]{0,1:T(8,128)(2,1)} %all-gather.5.cloned.1.call-done), kind=kOutput, calls=%fused_computation.2 | convolution fusion | flops 3356098560 | bytes 15728640 | tf_op jit(solution)/shard_map/btf,fd->btd/dot_general | solution.py:318
Async XLA Ops:
  6.5 1.9 copy-start
  6.5 42.2 %all-gather.3.cloned.1.call-start = ((), (), s32[]{:S(2)}) async-start(), calls=%async_computation | async-start | bytes 2048000 | tf_op jit(solution)/shard_map/all_gather | solution.py:279
  9.5 39.2 %copy-start.1 = (f32[640]{0:T(1024)S(1)}, f32[640]{0:T(1024)}, u32[]{:S(2)}) copy-start(f32[640]{0:T(1024)} %param.16) | copy-start | bytes 7684
  9.5 39.8 %copy-start.2 = (bf16[2,128,4]{1,2,0:T(4,128)(2,1)S(1)}, bf16[2,128,4]{1,2,0:T(4,128)(2,1)}, u32[]{:S(2)}) copy-start(bf16[2,128,4]{1,2,0:T(4,128)(2,1)} %param.12) | copy-start | bytes 6148
  11.5 212.5 %all-gather.5.cloned.1.call-start = ((), (), s32[]{:S(2)}) async-start(), calls=%async_computation.1 | async-start | bytes 14745600 | tf_op jit(solution)/shard_map/all_gather | solution.py:280
Sparse Core Ops, SparseCore 0:
  11.6 37.0 all-gather.2
  50.6 86.0 all-gather.4
where the time goes:
time: 241 us
  Pallas kernels  174 us (72%)
  waiting for transfers between devices  37.2 us (15%)
  between operations  13.4 us (6%)
  matrix products  9.77 us (4%)
  local copies, waits for them, and re-layouts  6.28 us (3%)
    pallas_call x1, Pallas kernels, per_device(): pl.pallas_call(functools.partial(kernel, n_ctx, n_head, rows), out_shape=...  174 us
    all_gather x1, waiting for transfers between devices, gather_proj(): piece = lax.all_gather(piece, 'head', axis=0, tiled=True)  37.1 us
    dot_general x1, matrix products, per_device(): jnp.einsum('btf,fd->btd', normed, proj, preferred_element_type=f32)  9.77 us
  transfers between devices with their start and end apart: 2, of which 1 were waited for; matrix products, arithmetic and copies ran while one was open for 1% of the time, Pallas kernels for 72%

commit v1 on v0

--- a/solution.py
+++ b/solution.py
@@ -28,13 +28,13 @@
 
 def kernel(
     n_ctx, n_head, rows,
-    q_ref, k_ref, v_ref, r_ref, g_ref, u_ref, d_ref, gain_ref,
+    q_ref, k_ref, v_ref, r_ref, kx0, tx0, w0, m0, gain_ref,
     o_ref,
-    tgt, kx, tx, qx, wb, wt, mst, gb, rb1, sb, rb2, dgu, hid, nrm,
+    tgt, kx, tx, qx, wb, mst, gb, rb1, sb, rb2, dgu, hid, nrm,
     tok_send, tok_recv, tok_local, rs1_s, rs1_r, rs2_s, rs2_r, ag_s, ag_r, sib_s, sib_r,
 ):
     blocks, share, _ = q_ref.shape
-    width = g_ref.shape[1]
+    width = w0.shape[1]
     chips = n_ctx // 2
     half = chips * rows
     me_c, me_z = lax.axis_index("ctx"), lax.axis_index("head")
@@ -94,20 +94,24 @@
             tgt[block, :, cols] = (v_ref[block, :, cols].astype(f32) * rate).astype(bf16)
 
     def grads(block):
+        kin = kx.at[block] if block else kx0
+        tin = tx.at[block] if block else tx0
+        win = wb.at[block] if block else w0
+
         def chunk(z, carry):
             at = pl.ds(pl.multiple_of(z * share, 16), share)
-            pre = dot(kx[block, z], wb[block, :2 * width, :], NT)
+            pre = dot(kin[z], win[:2 * width, :], NT)
             pre_gate, pre_up = pre[:, :width], pre[:, width:]
             sigma = jax.nn.sigmoid(pre_gate)
             silu = pre_gate * sigma
             hid[at, :] = silu * pre_up
-            back = dot(tx[block, z], wb[block, 2 * width:3 * width, :], NN)
+            back = dot(tin[z], win[2 * width:3 * width, :], NN)
             dgu[at, :width] = back * pre_up * sigma * (1.0 + pre_gate * (1.0 - sigma))
             dgu[at, width:] = back * silu
             return carry
 
         lax.fori_loop(0, n_head, chunk, 0)
-        keys = kx[block].reshape(n_head * share, width)
+        keys = kin[...].reshape(n_head * share, width)
 
         def key_tile(i, carry):
             at = pl.ds(pl.multiple_of(i * TILE, TILE), TILE)
@@ -115,14 +119,13 @@
             return carry
 
         lax.fori_loop(0, 2 * width // TILE, key_tile, 0)
-        targets = tx[block].reshape(n_head * share, width)
 
         def down_tile(i, carry):
             at = pl.ds(pl.multiple_of(i * TILE, TILE), TILE)
             to = pl.ds(pl.multiple_of(2 * width + i * TILE, TILE), TILE)
             high = hid[...].astype(bf16)
             low = (hid[...] - high.astype(f32)).astype(bf16)
-            tile = tx[block, :, :, at].reshape(n_head * share, TILE)
+            tile = tin[:, :, at].reshape(n_head * share, TILE)
             gb[block, to, :] = (dot(tile, high, TN) + dot(tile, low, TN)).astype(bf16)
             return carry
 
@@ -221,37 +224,28 @@
         local.start()
         return copies, local
 
-    key_sends = [spread(0, 0, k_ref, kx)]
-    scale_values(0)
-    tgt_sends = [spread(1, 0, tgt, tx)]
-    for block in range(1, blocks):
+    key_sends, tgt_sends = [None], [None]
+    if blocks > 1:
+        key_sends.append(spread(0, 1, k_ref, kx))
+        scale_values(1)
+        tgt_sends.append(spread(1, 1, tgt, tx))
+    for block in range(2, blocks):
         scale_values(block)
-    for index, ref in enumerate((g_ref, u_ref, d_ref)):
-        def turn(i, carry, ref=ref, index=index):
-            at = pl.ds(pl.multiple_of(i * TILE, TILE), TILE)
-            to = pl.ds(pl.multiple_of(index * width + i * TILE, TILE), TILE)
-            tile = ref[0, :, at].T
-            wt[to, :] = tile
-            wb[0, to, :] = tile.astype(bf16)
-            return carry
-
-        lax.fori_loop(0, width // TILE, turn, 0)
-    if n_ctx * rows > 3 * width:
-        wt[3 * width:, :] = jnp.zeros((n_ctx * rows - 3 * width, width), f32)
-    mst[...] = wt[mine, :]
+    mst[...] = m0[...]
     norm = jnp.sqrt(jnp.sum(mst[...] * mst[...], axis=1, keepdims=True))
 
     query_sends, results = [], []
     for block in range(blocks):
-        ahead = block + 1 < blocks
-        if ahead:
+        if block > 0:
+            ahead = block + 1 < blocks
             sent(key_sends[block])
-            key_sends.append(spread(0, block + 1, k_ref, kx))
-        arrived(key_sends[block])
-        if ahead:
+            if ahead:
+                key_sends.append(spread(0, block + 1, k_ref, kx))
+            arrived(key_sends[block])
             sent(tgt_sends[block])
-            tgt_sends.append(spread(1, block + 1, tgt, tx))
-        arrived(tgt_sends[block])
+            if ahead:
+                tgt_sends.append(spread(1, block + 1, tgt, tx))
+            arrived(tgt_sends[block])
         grads(block)
         state = reduce_start(block)
         if block > 0:
@@ -260,8 +254,6 @@
         state = reduce_finish(block, state, norm)
         query_sends.append(spread(2, block, q_ref, qx))
         share_finish(block, state)
-    sent(key_sends[-1])
-    sent(tgt_sends[-1])
     arrived(query_sends[-1])
     results.append(apply(blocks - 1))
     for copies in query_sends:
@@ -273,11 +265,63 @@
         copy.wait_send()
 
 
-def gather_proj(out_proj):
-    cols = out_proj.shape[1] // lax.axis_size("ctx")
-    piece = lax.dynamic_slice_in_dim(out_proj, lax.axis_index("ctx") * cols, cols, 1)
-    piece = lax.all_gather(piece, "head", axis=0, tiled=True)
-    return lax.all_gather(piece, "ctx", axis=1, tiled=True)
+def opening(
+    n_ctx, n_head, rows,
+    k_ref, v_ref, r_ref, g_ref, u_ref, d_ref,
+    kx0, tx0, w0, m0,
+    tgt, wt, send, recv, here,
+):
+    share = k_ref.shape[1]
+    width = g_ref.shape[1]
+    chips = n_ctx // 2
+    me_c, me_z = lax.axis_index("ctx"), lax.axis_index("head")
+
+    def peer(step):
+        return lax.rem(me_z + step, n_head)
+
+    def columns(head):
+        return pl.ds(pl.multiple_of(head * width, TILE), width)
+
+    barrier = pltpu.get_barrier_semaphore()
+    for step in range(1, n_head):
+        pl.semaphore_signal(barrier, inc=1, device_id={"head": peer(step)}, device_id_type=MESH)
+    pl.semaphore_wait(barrier, n_head - 1)
+    copies = []
+
+    def spread(kind, source, landing):
+        for step in range(1, n_head):
+            copies.append(pltpu.make_async_remote_copy(
+                src_ref=source.at[:, columns(peer(step))], dst_ref=landing.at[me_z],
+                send_sem=send.at[kind, step], recv_sem=recv.at[kind, step],
+                device_id={"head": peer(step)}, device_id_type=MESH,
+            ))
+            copies[-1].start()
+        copies.append(pltpu.make_async_copy(source.at[:, columns(me_z)], landing.at[me_z], here.at[kind]))
+        copies[-1].start()
+
+    spread(0, k_ref.at[0], kx0)
+    for head in range(n_head):
+        cols = slice(head * width, (head + 1) * width)
+        rate = r_ref[0, :, head:head + 1].astype(f32)
+        tgt[:, cols] = (v_ref[0, :, cols].astype(f32) * rate).astype(bf16)
+    spread(1, tgt, tx0)
+    for index, ref in enumerate((g_ref, u_ref, d_ref)):
+        def turn(i, carry, ref=ref, index=index):
+            at = pl.ds(pl.multiple_of(i * TILE, TILE), TILE)
+            to = pl.ds(pl.multiple_of(index * width + i * TILE, TILE), TILE)
+            tile = ref[0, :, at].T
+            wt[to, :] = tile
+            w0[to, :] = tile.astype(bf16)
+            return carry
+
+        lax.fori_loop(0, width // TILE, turn, 0)
+    if n_ctx * rows > 3 * width:
+        wt[3 * width:, :] = jnp.zeros((n_ctx * rows - 3 * width, width), f32)
+        w0[3 * width:, :] = jnp.zeros((n_ctx * rows - 3 * width, width), bf16)
+    own = lax.rem(me_c, 2) * chips + me_c // 2
+    m0[...] = wt[pl.ds(pl.multiple_of(own * rows, 16), rows), :]
+    for copy in copies:
+        copy.wait()
 
 
 def per_device(queries, keys, values, rates, gate_fast, up_fast, down_fast, out_gain, out_proj):
@@ -291,17 +335,40 @@
     exchange = pltpu.VMEM((blocks, chips, rows, width), bf16)
     vmem = pl.BlockSpec(memory_space=pltpu.VMEM)
     anywhere = pl.BlockSpec(memory_space=pl.ANY)
-    proj = gather_proj(out_proj)
+    cols = out_proj.shape[1] // n_ctx
+    piece = lax.dynamic_slice_in_dim(out_proj, lax.axis_index("ctx") * cols, cols, 1)
+    piece = lax.all_gather(piece, "head", axis=0, tiled=True)
+    arrivals = jax.ShapeDtypeStruct((n_head, share, width), bf16)
+    opened = pl.pallas_call(
+        functools.partial(opening, n_ctx, n_head, rows),
+        out_shape=[
+            arrivals, arrivals,
+            jax.ShapeDtypeStruct((n_ctx * rows, width), bf16),
+            jax.ShapeDtypeStruct((rows, width), f32),
+        ],
+        in_specs=[anywhere] + [vmem] * 5,
+        out_specs=[vmem] * 4,
+        scratch_shapes=[
+            pltpu.VMEM(values.shape[1:], bf16),
+            pltpu.VMEM((n_ctx * rows, width), f32),
+            dma((2, n_head)), dma((2, n_head)), dma((2,)),
+        ],
+        compiler_params=pltpu.CompilerParams(
+            collective_id=1, has_side_effects=True, vmem_limit_bytes=40 * 1024 * 1024
+        ),
+        cost_estimate=pl.CostEstimate(flops=0, bytes_accessed=120_000_000, transcendentals=0),
+    )(keys, values, rates, gate_fast, up_fast, down_fast)
+    opened, piece = lax.optimization_barrier((opened, piece))
+    proj = lax.all_gather(piece, "ctx", axis=1, tiled=True)
     normed = pl.pallas_call(
         functools.partial(kernel, n_ctx, n_head, rows),
         out_shape=jax.ShapeDtypeStruct(queries.shape, bf16),
-        in_specs=[anywhere] * 2 + [vmem] * 6,
+        in_specs=[anywhere] * 2 + [vmem] * 7,
         out_specs=vmem,
         scratch_shapes=[
             pltpu.VMEM(values.shape, bf16),
             landing, landing, landing,
             pltpu.VMEM((blocks + 1, n_ctx * rows, width), bf16),
-            pltpu.VMEM((n_ctx * rows, width), f32),
             pltpu.VMEM((rows, width), f32),
             pltpu.VMEM((blocks, n_ctx * rows, width), bf16),
             exchange, exchange, exchange,
@@ -314,7 +381,7 @@
             collective_id=0, has_side_effects=True, vmem_limit_bytes=60 * 1024 * 1024
         ),
         cost_estimate=pl.CostEstimate(flops=20_000_000_000, bytes_accessed=300_000_000, transcendentals=0),
-    )(queries, keys, values, rates, gate_fast, up_fast, down_fast, out_gain[None, :])
+    )(queries, keys, values, rates, *opened, out_gain[None, :])
     return jnp.einsum("btf,fd->btd", normed, proj, preferred_element_type=f32).astype(bf16)
 
 

time: 241 us -> 244 us (1.012)
  waiting for transfers between devices: 37.2 us -> 0.06 us
  Pallas kernels: 174 us -> 201 us
  local copies, waits for them, and re-layouts: 6.28 us -> 17.1 us
    pallas_call x0 -> x1, Pallas kernels: none -> 57.9 us  [per_device(): pl.pallas_call(functools.partial(opening, n_ctx, n_head, rows), out_shape...]
    all_gather x2, waiting for transfers between devices: 37.2 us -> 0.02 us  [the longest x1 0.02 us: per_device(): proj = lax.all_gather(piece, 'ctx', axis=1, tiled=True)]
    pallas_call x1, Pallas kernels: 174 us -> 143 us  [per_device(): pl.pallas_call(functools.partial(kernel, n_ctx, n_head, rows), out_shape=...]
    unnamed x8 -> x28, local copies, waits for them, and re-layouts: 4.67 us -> 15.5 us
  transfers between devices with their start and end apart: 2 -> 2, of which waited for: 1 -> 0; matrix products, arithmetic and copies ran while one was open for 1% -> 0% of each run, Pallas kernels for 72% -> 83%
where the time goes in v1:
time: 244 us; the launch traced here: 241 us
  Pallas kernels  201 us (82%)
  local copies, waits for them, and re-layouts  17.1 us (7%)
  between operations  13.5 us (6%)
  matrix products  9.77 us (4%)
    pallas_call x1, Pallas kernels, per_device(): pl.pallas_call(functools.partial(kernel, n_ctx, n_head, rows), out_shape=...  143 us
    pallas_call x1, Pallas kernels, per_device(): pl.pallas_call(functools.partial(opening, n_ctx, n_head, rows), out_shape...  57.9 us
    unnamed x28, local copies, waits for them, and re-layouts  15.5 us
    dot_general x1, matrix products, per_device(): jnp.einsum('btf,fd->btd', normed, proj, preferred_element_type=f32)  9.77 us
  transfers between devices with their start and end apart: 2, of which 0 were waited for; matrix products, arithmetic and copies ran while one was open for 0% of the time, Pallas kernels for 83%

profile of v1, /device:TPU:26, one launch (start us, length us, event | category | flops | bytes accessed | tf_op | source)
XLA Modules:
  0.0 241.4 jit_solution(7261573567267928657)
XLA Ops:
  6.5 0.0 copy-start
  6.5 0.0 copy-start.12
  6.5 0.0 all-gather.3.cloned.1.call-start
  6.5 1.9 copy-done
  8.5 1.0 constant_dynamic-slice_fusion
  9.5 2.0 copy.13
  11.4 0.0 all-gather.3.cloned.1.call-update
  11.5 0.0 all-gather.5.cloned.1.call-start
  11.5 0.0 copy-done.12
  11.5 0.1 copy.12.r_ref
  11.7 0.0 copy-start.1
  11.7 1.4 copy-done.1
  13.1 0.0 copy-start.2
  13.1 1.4 copy-done.2
  14.5 0.0 copy-start.3
  14.5 1.4 copy-done.3
  16.0 0.0 copy-start.4
  16.0 1.3 copy-done.4
  17.3 0.0 copy-start.5
  17.3 1.3 copy-done.5
  18.6 0.0 copy-start.6
  18.6 57.9 %shard_map.91 = (bf16[4,128,640]{2,1,0:T(8,128)(2,1)S(1)}, bf16[4,128,640]{2,1,0:T(8,128)(2,1)S(1)}, bf16[1920,640]{1,0:T(8,128)(2,1)S(1)}, f32[240,640]{1,0:T(8,128)S(1)}) custom-call(bf16[2,128,2560]{2,1,0:T(8,128)(2,1)S(1)} %copy-done.4, bf16[2,128,2560]{2,1,0:T(8,128)(2,1)S(1)} %copy-done.5, bf16[2,128,4]{2,1,0:T(8,128)(2,1)S(1)} %copy.12.r_ref, ...), custom_call_target="tpu_custom_call" | custom-call | bytes 120000000 | tf_op jit(solution)/shard_map/pallas_call | solution.py:342
  76.5 0.0 copy-done.6
  76.5 0.0 copy-start.7
  76.5 1.4 copy-done.7
  77.9 0.0 copy-start.8
  77.9 0.8 copy-done.8
  78.8 0.0 copy-start.9
  78.8 0.8 copy-done.9
  79.6 0.0 copy-start.10
  79.6 0.8 copy-done.10
  80.4 0.0 copy-start.11
  80.4 0.0 all-gather.3.cloned.1.call-done
  80.4 0.0 all-gather.5.cloned.1.call-update
  80.5 0.7 copy-done.11
  81.1 0.6 broadcast_in_dim.3.gain_ref
  81.7 143.1 %shard_map.92 = bf16[2,128,2560]{2,1,0:T(8,128)(2,1)} custom-call(bf16[2,128,2560]{2,1,0:T(8,128)(2,1)} %q_ref.1, bf16[2,128,2560]{2,1,0:T(8,128)(2,1)} %k_ref.3, bf16[2,128,2560]{2,1,0:T(8,128)(2,1)} %v_ref.3, bf16[2,128,4]{2,1,0:T(8,128)(2,1)} %copy-done.6, bf16[4,128,640]{2,1,0:T(8,128)(2,1)} %copy-done.8, bf16[4,128,640]{2,1,0:T(8,128)(2,1)} %copy-done.9, ...), custom_call_target="tpu_custom_call" | custom-call | flops 20000000000 | bytes 300000000 | tf_op jit(solution)/shard_map/pallas_call | solution.py:363
  224.8 0.0 all-gather.5.cloned.1.call-done
  224.8 9.8 %fusion.2 = bf16[2,128,2560]{2,1,0:T(8,128)(2,1)} fusion(bf16[2,128,2560]{2,1,0:T(8,128)(2,1)} %shard_map.92, bf16[2560,2560]{0,1:T(8,128)(2,1)} %all-gather.5.cloned.1.call-done), kind=kOutput, calls=%fused_computation.2 | convolution fusion | flops 3356098560 | bytes 15728640 | tf_op jit(solution)/shard_map/btf,fd->btd/dot_general | solution.py:385
Async XLA Ops:
  6.5 1.9 copy-start
  6.5 5.0 %copy-start.12 = (bf16[2,128,4]{1,2,0:T(4,128)(2,1)S(1)}, bf16[2,128,4]{1,2,0:T(4,128)(2,1)}, u32[]{:S(2)}) copy-start(bf16[2,128,4]{1,2,0:T(4,128)(2,1)} %param.12) | copy-start | bytes 6148
  6.5 73.9 %all-gather.3.cloned.1.call-start = ((), (), s32[]{:S(2)}) async-start(), calls=%async_computation | async-start | bytes 2048000 | tf_op jit(solution)/shard_map/all_gather | solution.py:340
  11.5 213.3 %all-gather.5.cloned.1.call-start = ((), (), s32[]{:S(2)}) async-start(), calls=%async_computation.1 | async-start | bytes 14745600 | tf_op jit(solution)/shard_map/all_gather | solution.py:362
  11.7 1.4 copy-start.1
  13.1 1.4 copy-start.2
  14.5 1.4 copy-start.3
  16.0 1.3 copy-start.4
  17.3 1.3 copy-start.5
  18.6 57.9 %copy-start.6 = (bf16[2,128,4]{2,1,0:T(8,128)(2,1)}, bf16[2,128,4]{2,1,0:T(8,128)(2,1)S(1)}, u32[]{:S(2)}) copy-start(bf16[2,128,4]{2,1,0:T(8,128)(2,1)S(1)} %copy.12.r_ref) | copy-start | bytes 6148
  76.5 1.4 copy-start.7
  77.9 0.8 copy-start.8
  78.8 0.8 copy-start.9
  79.6 0.8 copy-start.10
  80.4 0.7 copy-start.11
Sparse Core Ops, SparseCore 0:
  11.6 64.2 all-gather.2
  80.6 108.5 all-gather.4
